TPU v7x, 256 devices: a whole 4x4x8 slice. The times are simulated.
256 devices in a mesh: inp: 8 (over z), wgt: 8 (over x_lo, y), out: 4 (over x_hi, core).
Axes of the slice: x: 4 (x_hi: 2, x_lo: 2; x = x_hi * 2 + x_lo), y: 4, z: 8, core: 2. Of those that a mesh axis runs over, the one named last changes fastest.
Arguments:
- tokens: bfloat16 [1024, 6144], P('out', ('wgt', 'inp')), may hold values from -6 to 6
- w_up: bfloat16 [6144, 24576], P(('wgt', 'out'), 'inp'), may hold values from -0.078125 to 0.078125
- w_down: bfloat16 [24576, 6144], P(('inp', 'out'), 'wgt'), may hold values from -0.0390625 to 0.0390625
- grad_out: bfloat16 [1024, 6144], P('out', ('wgt', 'inp')), may hold values from -6 to 6
Outputs:
- output: bfloat16 [1024, 6144], P('out', ('wgt', 'inp'))
- grad_tokens: bfloat16 [1024, 6144], P('out', ('wgt', 'inp'))
- grad_up: bfloat16 [6144, 24576], P(('wgt', 'out'), 'inp')
- grad_down: bfloat16 [24576, 6144], P(('inp', 'out'), 'wgt')
All inputs are finite; a program needn't handle non-finite values.
Results may differ from a plain program's by a relative error of at most 0.029.
Values may be sent and summed in bfloat16 or wider, within the bound.
No kernel may reach another device: no remote copies, remote signals or barrier semaphores. Data moves between devices by JAX's collectives and lax.ppermute only.
A program may use at most 64 MiB of HBM per device.

v0:
```python
import jax
import jax.numpy as jnp
from jax import lax
from jax.sharding import PartitionSpec as P

tanh_scale = 0.7978845608028654
cubic_weight = 0.044715


def gelu_value(hidden):
    tangent = jnp.tanh(tanh_scale * (hidden + cubic_weight * hidden * hidden * hidden))
    return 0.5 * hidden * (1.0 + tangent)


def gelu_slope(hidden):
    tangent = jnp.tanh(tanh_scale * (hidden + cubic_weight * hidden * hidden * hidden))
    return 0.5 * (1.0 + tangent) + 0.5 * hidden * (1.0 - tangent * tangent) * tanh_scale * (
        1.0 + 3.0 * cubic_weight * hidden * hidden
    )


def product(former, latter):
    return jnp.dot(former, latter, preferred_element_type=jnp.float32)


def against(former, latter):
    return lax.dot_general(
        former, latter, (((1,), (1,)), ((), ())), preferred_element_type=jnp.float32
    )


def across(former, latter):
    return lax.dot_general(
        former, latter, (((0,), (0,)), ((), ())), preferred_element_type=jnp.float32
    )


def share_features(partial_value):
    return lax.psum_scatter(
        partial_value.astype(jnp.bfloat16), "inp", scatter_dimension=1, tiled=True
    ).astype(jnp.float32)


def share_hidden(partial_value):
    return lax.psum_scatter(
        partial_value.astype(jnp.bfloat16), "wgt", scatter_dimension=1, tiled=True
    ).astype(jnp.float32)


def whole_hidden(portion):
    return lax.all_gather(portion, "wgt", axis=1, tiled=True)


def weight_grad(former, latter):
    return lax.psum_scatter(
        across(former, latter).astype(jnp.bfloat16), "out", scatter_dimension=0, tiled=True
    ).astype(jnp.float32)


def per_device(tokens, w_up, w_down, grad_out):
    features, grad_features = (
        lax.all_gather(tokens, "inp", axis=1, tiled=True),
        lax.all_gather(grad_out, "inp", axis=1, tiled=True),
    )
    up_block, down_block = (
        lax.all_gather(w_up, "out", axis=0, tiled=True),
        lax.all_gather(w_down, "out", axis=0, tiled=True),
    )
    hidden_partial = product(features, up_block)
    hidden = share_hidden(hidden_partial)
    activation = whole_hidden(gelu_value(hidden).astype(jnp.bfloat16))
    output = share_features(product(activation, down_block)).astype(jnp.bfloat16)
    up_again, down_again = (
        lax.all_gather(w_up, "out", axis=0, tiled=True),
        lax.all_gather(w_down, "out", axis=0, tiled=True),
    )
    act_partial = against(grad_features, down_again)
    grad_act = share_hidden(act_partial)
    grad_hidden = whole_hidden((grad_act * gelu_slope(hidden)).astype(jnp.bfloat16))
    grad_tokens = share_features(against(grad_hidden, up_again)).astype(jnp.bfloat16)
    grad_down = weight_grad(activation, grad_features).astype(jnp.bfloat16)
    grad_up = weight_grad(features, grad_hidden).astype(jnp.bfloat16)
    return (output, grad_tokens, grad_up, grad_down)


def solution(mesh):
    placed = (
        P("out", ("wgt", "inp")),
        P(("wgt", "out"), "inp"),
        P(("inp", "out"), "wgt"),
        P("out", ("wgt", "inp")),
    )
    return jax.shard_map(
        per_device,
        mesh=mesh,
        in_specs=placed,
        out_specs=(
            P("out", ("wgt", "inp")),
            P("out", ("wgt", "inp")),
            P(("wgt", "out"), "inp"),
            P(("inp", "out"), "wgt"),
        ),
        check_vma=False,
    )
```

profile of v0, /device:TPU:1, one launch (start us, length us, event | category | flops | bytes accessed | tf_op | source)
XLA Modules:
  0.0 491.5 jit_solution(3880922465054088078)
XLA Ops:
  7.2 0.0 copy-start.2
  7.2 0.0 all-gather.9.cloned.1.call-start
  7.2 0.7 all-gather.9.cloned.1.call-update
  7.9 0.0 all-gather.5.cloned.1.call-start
  8.0 0.7 all-gather.5.cloned.1.call-update
  8.7 0.0 reduce-scatter.21.cloned.1.call-start
  8.7 0.0 copy-done.2
  8.7 23.7 %all_gather.24 = bf16[256,768]{0,1:T(8,128)(2,1)S(1)} all-gather(bf16[256,96]{0,1:T(8,128)(2,1)S(1)} %copy-done.2), channel_id=1, replica_groups=mesh['inp'=8,'wgt'=8,'out'=4] {'inp'}, dimensions={1}, use_global_device_ids=true | all-gather | bytes 442368 | tf_op jit(solution)/shard_map/all_gather | solution.py:63
  32.4 25.7 %all-gather.9.cloned.1.call-done = bf16[3072,768]{1,0:T(8,128)(2,1)} async-done(((bf16[768,768]{1,0:T(8,128)(2,1)}), bf16[3072,768]{1,0:T(8,128)(2,1)}) %all-gather.9.cloned.1.call-update) | async-done | bytes 4718608 | tf_op jit(solution)/shard_map/all_gather | solution.py:67
  58.1 3.8 convolution_convert_fusion.2
  61.9 1.6 copy.12
  63.5 0.0 copy-start.3
  63.5 0.0 reduce-scatter.21.cloned.1.call-update
  63.5 0.0 reduce-scatter.19.cloned.1.call-start
  63.5 0.7 copy-done.3
  64.3 21.4 %all_gather.20 = bf16[256,768]{0,1:T(8,128)(2,1)S(1)} all-gather(bf16[256,96]{0,1:T(8,128)(2,1)S(1)} %copy-done.3), channel_id=1, replica_groups=mesh['inp'=8,'wgt'=8,'out'=4] {'inp'}, dimensions={1}, use_global_device_ids=true | all-gather | bytes 442368 | tf_op jit(solution)/shard_map/all_gather | solution.py:62
  85.6 17.8 %all-gather.5.cloned.1.call-done = bf16[768,3072]{1,0:T(8,128)(2,1)} async-done(((bf16[192,3072]{1,0:T(8,128)(2,1)}), bf16[768,3072]{1,0:T(8,128)(2,1)}) %all-gather.5.cloned.1.call-update) | async-done | bytes 4718608 | tf_op jit(solution)/shard_map/all_gather | solution.py:66
  103.5 3.7 convolution_convert_fusion.3
  107.2 1.6 copy.10
  108.8 0.0 reduce-scatter.19.cloned.1.call-update
  108.8 0.0 all-gather.11.cloned.1.call-start
  108.9 34.6 %reduce-scatter.21.cloned.1.call-done = bf16[384,256]{1,0:T(8,128)(2,1)} async-done(((bf16[3072,256]{1,0:T(8,128)(2,1)}), bf16[384,256]{1,0:T(8,128)(2,1)}) %reduce-scatter.21.cloned.1.call-update) | async-done | bytes 196624
  143.5 1.1 copy.13
  144.6 43.6 %reduce-scatter.19.cloned.1.call-done = bf16[384,256]{1,0:T(8,128)(2,1)} async-done(((bf16[3072,256]{1,0:T(8,128)(2,1)}), bf16[384,256]{1,0:T(8,128)(2,1)}) %reduce-scatter.19.cloned.1.call-update) | async-done | bytes 196624
  188.2 1.1 copy.11
  189.3 1.0 fusion.8
  190.3 0.0 all-gather.11.cloned.1.call-update
  190.4 0.0 all-gather.7.cloned.1.call-start
  190.4 0.5 all-gather.7.cloned.1.call-update
  190.9 0.0 reduce-scatter.15.cloned.1.call-start
  191.0 40.2 %all-gather.11.cloned.1.call-done = bf16[256,3072]{1,0:T(8,128)(2,1)} async-done(((bf16[256,384]{1,0:T(8,128)(2,1)}), bf16[256,3072]{1,0:T(8,128)(2,1)}) %all-gather.11.cloned.1.call-update) | async-done | bytes 1572880 | tf_op jit(solution)/shard_map/all_gather | solution.py:51
  231.2 5.0 %convolution_convert_fusion.4 = bf16[256,768]{0,1:T(8,128)(2,1)} fusion(bf16[256,3072]{1,0:T(8,128)(2,1)} %all-gather.11.cloned.1.call-done, bf16[768,3072]{1,0:T(8,128)(2,1)} %all-gather.5.cloned.1.call-done), kind=kOutput, calls=%fused_computation.5 | convolution fusion | flops 1208156160 | bytes 6684672 | tf_op jit(solution)/shard_map/dot_general | solution.py:27
  236.1 0.0 reduce-scatter.15.cloned.1.call-update
  236.2 0.0 reduce-scatter.13.cloned.1.call-start
  236.2 39.3 %all-gather.7.cloned.1.call-done = bf16[256,3072]{1,0:T(8,128)(2,1)} async-done(((bf16[256,384]{1,0:T(8,128)(2,1)}), bf16[256,3072]{1,0:T(8,128)(2,1)}) %all-gather.7.cloned.1.call-update) | async-done | bytes 1572880 | tf_op jit(solution)/shard_map/all_gather | solution.py:51
  275.5 0.0 copy-start.1
  275.5 5.6 %convolution_convert_fusion.5 = bf16[256,768]{0,1:T(8,128)(2,1)} fusion(bf16[256,3072]{1,0:T(8,128)(2,1)} %all-gather.7.cloned.1.call-done, bf16[3072,768]{1,0:T(8,128)(2,1)} %all-gather.9.cloned.1.call-done), kind=kOutput, calls=%fused_computation.6 | convolution fusion | flops 1208156160 | bytes 6684672 | tf_op jit(solution)/shard_map/dot_general | solution.py:23
  281.2 0.0 reduce-scatter.13.cloned.1.call-update
  281.2 0.0 reduce-scatter.17.cloned.1.call-start
  281.3 0.0 copy-done.1
  281.3 3.6 convolution_convert_fusion
  284.8 0.0 copy-start
  284.8 0.0 reduce-scatter.17.cloned.1.call-update
  284.9 0.0 reduce-scatter.23.cloned.1.call-start
  284.9 1.3 copy-done
  286.2 3.7 fusion
  289.9 6.7 %copy.14 = bf16[768,3072]{1,0:T(8,128)(2,1)} copy(bf16[768,3072]{0,1:T(8,128)(2,1)} %fusion) | data formatting | bytes 9437184
  296.6 0.0 reduce-scatter.23.cloned.1.call-update
  296.7 19.6 %reduce-scatter.15.cloned.1.call-done = bf16[256,96]{0,1:T(8,128)(2,1)} async-done(((bf16[256,768]{0,1:T(8,128)(2,1)}), bf16[256,96]{0,1:T(8,128)(2,1)}) %reduce-scatter.15.cloned.1.call-update) | async-done | bytes 49168 | tf_op jit(solution)/shard_map/reduce_scatter | solution.py:39
  316.3 38.9 %reduce-scatter.13.cloned.1.call-done = bf16[256,96]{0,1:T(8,128)(2,1)} async-done(((bf16[256,768]{0,1:T(8,128)(2,1)}), bf16[256,96]{0,1:T(8,128)(2,1)}) %reduce-scatter.13.cloned.1.call-update) | async-done | bytes 49168 | tf_op jit(solution)/shard_map/reduce_scatter | solution.py:39
  355.2 66.7 %reduce-scatter.17.cloned.1.call-done = bf16[768,768]{1,0:T(8,128)(2,1)} async-done(((bf16[3072,768]{1,0:T(8,128)(2,1)}), bf16[768,768]{1,0:T(8,128)(2,1)}) %reduce-scatter.17.cloned.1.call-update) | async-done | bytes 1179664 | tf_op jit(solution)/shard_map/reduce_scatter | solution.py:55
  421.9 62.8 %reduce-scatter.23.cloned.1.call-done = bf16[192,3072]{1,0:T(8,128)(2,1)} async-done(((bf16[768,3072]{1,0:T(8,128)(2,1)}), bf16[192,3072]{1,0:T(8,128)(2,1)}) %reduce-scatter.23.cloned.1.call-update) | async-done | bytes 1179664
Async XLA Ops:
  7.2 1.5 copy-start.2
  7.2 50.9 %all-gather.9.cloned.1.call-start = ((), (), s32[]{:S(2)}) async-start(), calls=%async_computation.8 | async-start | bytes 5898240 | tf_op jit(solution)/shard_map/all_gather | solution.py:67
  7.9 95.6 %all-gather.5.cloned.1.call-start = ((), (), s32[]{:S(2)}) async-start(), calls=%async_computation.6 | async-start | bytes 5898240 | tf_op jit(solution)/shard_map/all_gather | solution.py:66
  8.7 134.8 %reduce-scatter.21.cloned.1.call-start = ((), (), s32[]{:S(2)}) async-start(), calls=%async_computation.14 | async-start | bytes 1769472
  63.5 0.8 copy-start.3
  63.5 124.7 %reduce-scatter.19.cloned.1.call-start = ((), (), s32[]{:S(2)}) async-start(), calls=%async_computation.13 | async-start | bytes 1769472
  108.8 122.4 %all-gather.11.cloned.1.call-start = ((), (), s32[]{:S(2)}) async-start(), calls=%async_computation.10 | async-start | bytes 1769472 | tf_op jit(solution)/shard_map/all_gather | solution.py:51
  190.4 85.2 %all-gather.7.cloned.1.call-start = ((), (), s32[]{:S(2)}) async-start(), calls=%async_computation.7 | async-start | bytes 1769472 | tf_op jit(solution)/shard_map/all_gather | solution.py:51
  190.9 125.4 %reduce-scatter.15.cloned.1.call-start = ((), (), s32[]{:S(2)}) async-start(), calls=%async_computation.11 | async-start | bytes 442368 | tf_op jit(solution)/shard_map/reduce_scatter | solution.py:39
  236.2 119.1 %reduce-scatter.13.cloned.1.call-start = ((), (), s32[]{:S(2)}) async-start(), calls=%async_computation.9 | async-start | bytes 442368 | tf_op jit(solution)/shard_map/reduce_scatter | solution.py:39
  275.5 5.7 %copy-start.1 = (bf16[256,3072]{1,0:T(8,128)(2,1)S(1)}, bf16[256,3072]{1,0:T(8,128)(2,1)}, u32[]{:S(2)}) copy-start(bf16[256,3072]{1,0:T(8,128)(2,1)} %all-gather.7.cloned.1.call-done) | copy-start | bytes 4718596
  281.2 140.7 %reduce-scatter.17.cloned.1.call-start = ((), (), s32[]{:S(2)}) async-start(), calls=%async_computation.12 | async-start | bytes 5898240 | tf_op jit(solution)/shard_map/reduce_scatter | solution.py:55
  284.8 1.4 copy-start
  284.9 199.8 %reduce-scatter.23.cloned.1.call-start = ((), (), s32[]{:S(2)}) async-start(), calls=%async_computation.15 | async-start | bytes 5898240
Sparse Core Ops, SparseCore 0:
  9.8 48.2 all-gather.8
  59.9 43.5 all-gather.4
  106.0 37.3 reduce-scatter.20
  145.9 42.2 reduce-scatter.18
  190.5 40.6 all-gather.10
  233.4 42.0 all-gather.6
  278.6 37.6 reduce-scatter.14
  319.5 35.6 reduce-scatter.12
  358.6 63.2 reduce-scatter.16
  425.3 59.3 reduce-scatter.22
where the time goes:
time: 492 us
  waiting for transfers between devices  391 us (79%)
  blocking collectives  45.1 us (9%)
  matrix products  25.4 us (5%)
  between operations  14.2 us (3%)
  local copies, waits for them, and re-layouts  14.1 us (3%)
    unnamed x13, waiting for transfers between devices  143 us
    all_gather x2, waiting for transfers between devices, whole_hidden(): return lax.all_gather(portion, 'wgt', axis=1, tiled=True)  79.5 us
    reduce_scatter x1, waiting for transfers between devices, weight_grad(): lax.psum_scatter(across(former, latter).astype(jnp.bfloat16), 'out', scat...  66.7 us
    reduce_scatter x2, waiting for transfers between devices, share_features(): lax.psum_scatter(partial_value.astype(jnp.bfloat16), 'inp', scatter_dimen...  58.6 us
    all_gather x1, waiting for transfers between devices, per_device(): lax.all_gather(w_down, 'out', axis=0, tiled=True)  25.7 us
    all_gather x1, blocking collectives, per_device(): lax.all_gather(grad_out, 'inp', axis=1, tiled=True)  23.7 us
    all_gather x1, blocking collectives, per_device(): lax.all_gather(tokens, 'inp', axis=1, tiled=True)  21.4 us
    all_gather x1, waiting for transfers between devices, per_device(): lax.all_gather(w_up, 'out', axis=0, tiled=True)  17.8 us
  transfers between devices with their start and end apart: 10, of which 10 were waited for; matrix products, arithmetic and copies ran while one was open for 7% of the time, Pallas kernels for 0%

commit v1 on v0

--- a/solution.py
+++ b/solution.py
@@ -1,10 +1,27 @@
+import functools
 import jax
 import jax.numpy as jnp
 from jax import lax
 from jax.sharding import PartitionSpec as P
+from jax.lax import all_to_all, axis_size
 
 tanh_scale = 0.7978845608028654
 cubic_weight = 0.044715
+
+
+def _group_rows(unit, axis_name):
+    return jnp.concatenate(
+        all_to_all(
+            jnp.stack([unit] * axis_size(axis_name), 0),
+            axis_name=axis_name,
+            split_axis=0,
+            concat_axis=0,
+        ),
+        1,
+    )
+
+
+_time_heads = functools.partial(_group_rows, axis_name="inp")
 
 
 def gelu_value(hidden):
@@ -60,7 +77,7 @@
 def per_device(tokens, w_up, w_down, grad_out):
     features, grad_features = (
         lax.all_gather(tokens, "inp", axis=1, tiled=True),
-        lax.all_gather(grad_out, "inp", axis=1, tiled=True),
+        _time_heads(grad_out),
     )
     up_block, down_block = (
         lax.all_gather(w_up, "out", axis=0, tiled=True),

time: 492 us -> 492 us (level)
    all_gather x1 -> x0, blocking collectives: 23.7 us -> none  [per_device(): lax.all_gather(grad_out, 'inp', axis=1, tiled=True)]
    all_to_all x0 -> x1, blocking collectives: none -> 22.3 us  [_group_rows(): all_to_all(jnp.stack([unit] * axis_size(axis_name), 0), axis_name=axis_na...]
where the time goes in v1:
time: 492 us
  waiting for transfers between devices  393 us (80%)
  blocking collectives  43.7 us (9%)
  matrix products  25.4 us (5%)
  between operations  14.2 us (3%)
  local copies, waits for them, and re-layouts  14.1 us (3%)
    unnamed x13, waiting for transfers between devices  143 us
    all_gather x2, waiting for transfers between devices, whole_hidden(): return lax.all_gather(portion, 'wgt', axis=1, tiled=True)  79.5 us
    reduce_scatter x1, waiting for transfers between devices, weight_grad(): lax.psum_scatter(across(former, latter).astype(jnp.bfloat16), 'out', scat...  66.7 us
    reduce_scatter x2, waiting for transfers between devices, share_features(): lax.psum_scatter(partial_value.astype(jnp.bfloat16), 'inp', scatter_dimen...  58.6 us
    all_gather x1, waiting for transfers between devices, per_device(): lax.all_gather(w_down, 'out', axis=0, tiled=True)  27 us
    all_to_all x1, blocking collectives, _group_rows(): all_to_all(jnp.stack([unit] * axis_size(axis_name), 0), axis_name=axis_na...  22.3 us
    all_gather x1, blocking collectives, per_device(): lax.all_gather(tokens, 'inp', axis=1, tiled=True)  21.4 us
    all_gather x1, waiting for transfers between devices, per_device(): lax.all_gather(w_up, 'out', axis=0, tiled=True)  17.8 us
  transfers between devices with their start and end apart: 10, of which 10 were waited for; matrix products, arithmetic and copies ran while one was open for 7% of the time, Pallas kernels for 0%

profile of v1, /device:TPU:1, one launch (start us, length us, event | category | flops | bytes accessed | tf_op | source)
XLA Modules:
  0.0 491.5 jit_solution(1685771545222904754)
XLA Ops:
  7.2 0.0 copy-start.2
  7.2 0.0 all-gather.9.cloned.1.call-start
  7.2 0.7 all-gather.9.cloned.1.call-update
  7.9 0.0 all-gather.5.cloned.1.call-start
  8.0 0.7 all-gather.5.cloned.1.call-update
  8.7 0.0 reduce-scatter.21.cloned.1.call-start
  8.7 0.0 copy-done.2
  8.7 22.3 %all_to_all.5 = bf16[8,256,96]{1,2,0:T(8,128)(2,1)S(1)} all-to-all(bf16[8,256,96]{1,2,0:T(8,128)(2,1)S(1)} %stack.2), channel_id=1, replica_groups=mesh['inp'=8,'wgt'=8,'out'=4] {'inp'}, dimensions={0} | all-to-all | bytes 786432 | tf_op jit(solution)/shard_map/all_to_all | solution.py:14
  31.1 27.0 %all-gather.9.cloned.1.call-done = bf16[3072,768]{1,0:T(8,128)(2,1)} async-done(((bf16[768,768]{1,0:T(8,128)(2,1)}), bf16[3072,768]{1,0:T(8,128)(2,1)}) %all-gather.9.cloned.1.call-update) | async-done | bytes 4718608 | tf_op jit(solution)/shard_map/all_gather | solution.py:84
  58.1 3.8 convolution_convert_fusion.2
  61.9 1.6 copy.14
  63.5 0.0 copy-start.3
  63.5 0.0 reduce-scatter.21.cloned.1.call-update
  63.5 0.0 reduce-scatter.19.cloned.1.call-start
  63.5 0.7 copy-done.3
  64.3 21.4 %all_gather.17 = bf16[256,768]{0,1:T(8,128)(2,1)S(1)} all-gather(bf16[256,96]{0,1:T(8,128)(2,1)S(1)} %copy-done.3), channel_id=1, replica_groups=mesh['inp'=8,'wgt'=8,'out'=4] {'inp'}, dimensions={1}, use_global_device_ids=true | all-gather | bytes 442368 | tf_op jit(solution)/shard_map/all_gather | solution.py:79
  85.6 17.8 %all-gather.5.cloned.1.call-done = bf16[768,3072]{1,0:T(8,128)(2,1)} async-done(((bf16[192,3072]{1,0:T(8,128)(2,1)}), bf16[768,3072]{1,0:T(8,128)(2,1)}) %all-gather.5.cloned.1.call-update) | async-done | bytes 4718608 | tf_op jit(solution)/shard_map/all_gather | solution.py:83
  103.5 3.7 convolution_convert_fusion.3
  107.2 1.6 copy.12
  108.8 0.0 reduce-scatter.19.cloned.1.call-update
  108.8 0.0 all-gather.11.cloned.1.call-start
  108.9 34.6 %reduce-scatter.21.cloned.1.call-done = bf16[384,256]{1,0:T(8,128)(2,1)} async-done(((bf16[3072,256]{1,0:T(8,128)(2,1)}), bf16[384,256]{1,0:T(8,128)(2,1)}) %reduce-scatter.21.cloned.1.call-update) | async-done | bytes 196624
  143.5 1.1 copy.15
  144.6 43.6 %reduce-scatter.19.cloned.1.call-done = bf16[384,256]{1,0:T(8,128)(2,1)} async-done(((bf16[3072,256]{1,0:T(8,128)(2,1)}), bf16[384,256]{1,0:T(8,128)(2,1)}) %reduce-scatter.19.cloned.1.call-update) | async-done | bytes 196624
  188.2 1.1 copy.13
  189.3 1.0 fusion.8
  190.3 0.0 all-gather.11.cloned.1.call-update
  190.4 0.0 all-gather.7.cloned.1.call-start
  190.4 0.5 all-gather.7.cloned.1.call-update
  190.9 0.0 reduce-scatter.15.cloned.1.call-start
  191.0 40.2 %all-gather.11.cloned.1.call-done = bf16[256,3072]{1,0:T(8,128)(2,1)} async-done(((bf16[256,384]{1,0:T(8,128)(2,1)}), bf16[256,3072]{1,0:T(8,128)(2,1)}) %all-gather.11.cloned.1.call-update) | async-done | bytes 1572880 | tf_op jit(solution)/shard_map/all_gather | solution.py:68
  231.2 5.0 %convolution_convert_fusion.4 = bf16[256,768]{0,1:T(8,128)(2,1)} fusion(bf16[256,3072]{1,0:T(8,128)(2,1)} %all-gather.11.cloned.1.call-done, bf16[768,3072]{1,0:T(8,128)(2,1)} %all-gather.5.cloned.1.call-done), kind=kOutput, calls=%fused_computation.5 | convolution fusion | flops 1208156160 | bytes 6684672 | tf_op jit(solution)/shard_map/dot_general | solution.py:44
  236.1 0.0 reduce-scatter.15.cloned.1.call-update
  236.2 0.0 reduce-scatter.13.cloned.1.call-start
  236.2 39.3 %all-gather.7.cloned.1.call-done = bf16[256,3072]{1,0:T(8,128)(2,1)} async-done(((bf16[256,384]{1,0:T(8,128)(2,1)}), bf16[256,3072]{1,0:T(8,128)(2,1)}) %all-gather.7.cloned.1.call-update) | async-done | bytes 1572880 | tf_op jit(solution)/shard_map/all_gather | solution.py:68
  275.5 0.0 copy-start.1
  275.5 5.6 %convolution_convert_fusion.5 = bf16[256,768]{0,1:T(8,128)(2,1)} fusion(bf16[256,3072]{1,0:T(8,128)(2,1)} %all-gather.7.cloned.1.call-done, bf16[3072,768]{1,0:T(8,128)(2,1)} %all-gather.9.cloned.1.call-done), kind=kOutput, calls=%fused_computation.6 | convolution fusion | flops 1208156160 | bytes 6684672 | tf_op jit(solution)/shard_map/dot_general | solution.py:40
  281.2 0.0 reduce-scatter.13.cloned.1.call-update
  281.2 0.0 reduce-scatter.17.cloned.1.call-start
  281.3 0.0 copy-done.1
  281.3 3.6 convolution_convert_fusion
  284.8 0.0 copy-start
  284.8 0.0 reduce-scatter.17.cloned.1.call-update
  284.9 0.0 reduce-scatter.23.cloned.1.call-start
  284.9 1.3 copy-done
  286.2 3.7 fusion
  289.9 6.7 %copy.16 = bf16[768,3072]{1,0:T(8,128)(2,1)} copy(bf16[768,3072]{0,1:T(8,128)(2,1)} %fusion) | data formatting | bytes 9437184
  296.6 0.0 reduce-scatter.23.cloned.1.call-update
  296.7 19.6 %reduce-scatter.15.cloned.1.call-done = bf16[256,96]{0,1:T(8,128)(2,1)} async-done(((bf16[256,768]{0,1:T(8,128)(2,1)}), bf16[256,96]{0,1:T(8,128)(2,1)}) %reduce-scatter.15.cloned.1.call-update) | async-done | bytes 49168 | tf_op jit(solution)/shard_map/reduce_scatter | solution.py:56
  316.3 38.9 %reduce-scatter.13.cloned.1.call-done = bf16[256,96]{0,1:T(8,128)(2,1)} async-done(((bf16[256,768]{0,1:T(8,128)(2,1)}), bf16[256,96]{0,1:T(8,128)(2,1)}) %reduce-scatter.13.cloned.1.call-update) | async-done | bytes 49168 | tf_op jit(solution)/shard_map/reduce_scatter | solution.py:56
  355.2 66.7 %reduce-scatter.17.cloned.1.call-done = bf16[768,768]{1,0:T(8,128)(2,1)} async-done(((bf16[3072,768]{1,0:T(8,128)(2,1)}), bf16[768,768]{1,0:T(8,128)(2,1)}) %reduce-scatter.17.cloned.1.call-update) | async-done | bytes 1179664 | tf_op jit(solution)/shard_map/reduce_scatter | solution.py:72
  421.9 62.8 %reduce-scatter.23.cloned.1.call-done = bf16[192,3072]{1,0:T(8,128)(2,1)} async-done(((bf16[768,3072]{1,0:T(8,128)(2,1)}), bf16[192,3072]{1,0:T(8,128)(2,1)}) %reduce-scatter.23.cloned.1.call-update) | async-done | bytes 1179664
  (1 shorter events, 0.0 us)
Async XLA Ops:
  7.2 1.5 copy-start.2
  7.2 50.9 %all-gather.9.cloned.1.call-start = ((), (), s32[]{:S(2)}) async-start(), calls=%async_computation.9 | async-start | bytes 5898240 | tf_op jit(solution)/shard_map/all_gather | solution.py:84
  7.9 95.6 %all-gather.5.cloned.1.call-start = ((), (), s32[]{:S(2)}) async-start(), calls=%async_computation.7 | async-start | bytes 5898240 | tf_op jit(solution)/shard_map/all_gather | solution.py:83
  8.7 134.8 %reduce-scatter.21.cloned.1.call-start = ((), (), s32[]{:S(2)}) async-start(), calls=%async_computation.15 | async-start | bytes 1769472
  63.5 0.8 copy-start.3
  63.5 124.7 %reduce-scatter.19.cloned.1.call-start = ((), (), s32[]{:S(2)}) async-start(), calls=%async_computation.14 | async-start | bytes 1769472
  108.8 122.4 %all-gather.11.cloned.1.call-start = ((), (), s32[]{:S(2)}) async-start(), calls=%async_computation.11 | async-start | bytes 1769472 | tf_op jit(solution)/shard_map/all_gather | solution.py:68
  190.4 85.2 %all-gather.7.cloned.1.call-start = ((), (), s32[]{:S(2)}) async-start(), calls=%async_computation.8 | async-start | bytes 1769472 | tf_op jit(solution)/shard_map/all_gather | solution.py:68
  190.9 125.4 %reduce-scatter.15.cloned.1.call-start = ((), (), s32[]{:S(2)}) async-start(), calls=%async_computation.12 | async-start | bytes 442368 | tf_op jit(solution)/shard_map/reduce_scatter | solution.py:56
  236.2 119.1 %reduce-scatter.13.cloned.1.call-start = ((), (), s32[]{:S(2)}) async-start(), calls=%async_computation.10 | async-start | bytes 442368 | tf_op jit(solution)/shard_map/reduce_scatter | solution.py:56
  275.5 5.7 %copy-start.1 = (bf16[256,3072]{1,0:T(8,128)(2,1)S(1)}, bf16[256,3072]{1,0:T(8,128)(2,1)}, u32[]{:S(2)}) copy-start(bf16[256,3072]{1,0:T(8,128)(2,1)} %all-gather.7.cloned.1.call-done) | copy-start | bytes 4718596
  281.2 140.7 %reduce-scatter.17.cloned.1.call-start = ((), (), s32[]{:S(2)}) async-start(), calls=%async_computation.13 | async-start | bytes 5898240 | tf_op jit(solution)/shard_map/reduce_scatter | solution.py:72
  284.8 1.4 copy-start
  284.9 199.8 %reduce-scatter.23.cloned.1.call-start = ((), (), s32[]{:S(2)}) async-start(), calls=%async_computation.16 | async-start | bytes 5898240
Sparse Core Ops, SparseCore 0:
  9.8 48.2 all-gather.8
  59.9 43.5 all-gather.4
  106.0 37.3 reduce-scatter.20
  145.9 42.2 reduce-scatter.18
  190.5 40.6 all-gather.10
  233.4 42.0 all-gather.6
  278.6 37.6 reduce-scatter.14
  319.5 35.6 reduce-scatter.12
  358.6 63.2 reduce-scatter.16
  425.3 59.3 reduce-scatter.22
